TPU v7x, 32 devices: a whole 2x2x4 slice. The times are simulated.
32 devices in a mesh: replica: 2 (over x), fsdp: 16 (over z, y, core).
Axes of the slice: x: 2, y: 2, z: 4, core: 2. Of those that a mesh axis runs over, the one named last changes fastest.
Arguments:
- tokens_in: bfloat16 [4, 32, 197, 384], P(None, ('replica', 'fsdp')), may hold values from -6 to 6
- picks_in: int32 [4, 32, 197, 2], P(None, ('replica', 'fsdp')), may hold values from 0 to 31, all different within a row
- ranks_in: int32 [4, 32, 197], P(None, ('replica', 'fsdp')), may hold values from 0 to 196, each once within a row
- capacity: int32 [32], replicated, may hold values from 9 to 16, as said below
- first_gain: bfloat16 [384], P('fsdp'), may hold values from 0.5 to 1.5
- first_shift: bfloat16 [384], P('fsdp'), may hold values from -1 to 1
- attend_weight: bfloat16 [384, 1152], P('fsdp'), may hold values from -0.3125 to 0.3125
- output_weight: bfloat16 [384, 384], P('fsdp'), may hold values from -1.21875 to 1.21875
- second_gain: bfloat16 [384], P('fsdp'), may hold values from 0.5 to 1.5
- second_shift: bfloat16 [384], P('fsdp'), may hold values from -1 to 1
- router_weight: bfloat16 [384, 32], P('fsdp'), may hold values from -0.21386719 to 0.21386719
- expert_up: bfloat16 [32, 384, 1536], P('fsdp'), may hold values from -0.3125 to 0.3125
- expert_down: bfloat16 [32, 1536, 384], P('fsdp'), may hold values from -3.671875 to 3.671875
- cotangent: bfloat16 [4, 32, 197, 384], P(None, ('replica', 'fsdp')), may hold values from -6 to 6
Outputs:
- block_out: bfloat16 [4, 32, 197, 384], P(None, ('replica', 'fsdp'))
- input_gradient: bfloat16 [4, 32, 197, 384], P(None, ('replica', 'fsdp'))
- first_gain_gradient: float32 [384], P('fsdp')
- first_shift_gradient: float32 [384], P('fsdp')
- attend_gradient: float32 [384, 1152], P('fsdp')
- output_gradient: float32 [384, 384], P('fsdp')
- second_gain_gradient: float32 [384], P('fsdp')
- second_shift_gradient: float32 [384], P('fsdp')
- router_gradient: float32 [384, 32], P('fsdp')
- expert_up_gradient: float32 [32, 384, 1536], P('fsdp')
- expert_down_gradient: float32 [32, 1536, 384], P('fsdp')
Inputs may be any that keep to these rules, and one draw needn't show every extreme that they name: `picks_in`: each row names two different experts. `ranks_in`: within an image the ranks are the numbers 0 to 196, each once. `capacity`: some expert has exactly 16.
All inputs are finite; a program needn't handle non-finite values.
Results may differ from a plain program's by a relative error of at most 0.022.
Values may be sent and summed in bfloat16 or wider, within the bound.
No kernel may reach another device: no remote copies, remote signals or barrier semaphores. Data moves between devices by JAX's collectives and lax.ppermute only.
A program may use at most 128 MiB of HBM per device.

v0:
```python
import jax
import jax.numpy as jnp
from jax import lax
from jax.sharding import PartitionSpec as P

HEADS = 6
HEAD_DIM = 64
CAP = 16


EPSILON = 1e-06


def layer_norm(values, gain, shift):
    center = values - jnp.mean(values, axis=-1, keepdims=True)
    spread = jnp.mean(center * center, axis=-1, keepdims=True)
    return center * lax.rsqrt(spread + EPSILON) * gain + shift


def route(picks, ranks, capacity):
    length = picks.shape[0]
    experts = jnp.concatenate([picks[:, 0], picks[:, 1]])
    order = jnp.concatenate([ranks, ranks + length])
    same = experts[:, None] == experts[None, :]
    earlier = order[None, :] < order[:, None]
    position = jnp.sum((same & earlier).astype(jnp.int32), axis=1)
    labels = jnp.arange(capacity.shape[0], dtype=jnp.int32)
    limit = jnp.sum(jnp.where(experts[:, None] == labels[None, :], capacity[None, :], 0), axis=1)
    kept = position < limit
    slot = jnp.where(kept, experts * CAP + position, 0)
    return (slot.reshape(2, length).T, kept.reshape(2, length).T)


def contract_rows(left, right):
    return lax.dot_general(
        left, right, (((0,), (0,)), ((), ())), preferred_element_type=jnp.float32
    )


def contract_cols(left, right):
    return lax.dot_general(
        left, right, (((1,), (1,)), ((), ())), preferred_element_type=jnp.float32
    )


def body(
    tokens_in,
    picks_in,
    ranks_in,
    capacity,
    first_gain,
    first_shift,
    attend_weight,
    output_weight,
    second_gain,
    second_shift,
    router_weight,
    expert_up,
    expert_down,
    cotangent,
):
    micro = tokens_in.shape[0]
    length = tokens_in.shape[2]
    width = tokens_in.shape[3]
    experts = capacity.shape[0]
    groups = lax.axis_size("fsdp")
    local_experts = expert_up.shape[0]
    scale = HEAD_DIM ** (-0.5)
    slots = experts * CAP
    shard_list = (
        first_gain,
        first_shift,
        attend_weight,
        output_weight,
        second_gain,
        second_shift,
        router_weight,
    )
    totals = tuple(
        (
            jnp.zeros((piece.shape[0] * groups,) + piece.shape[1:], jnp.float32)
            for piece in shard_list
        )
    )
    up_total = jnp.zeros(expert_up.shape, jnp.float32)
    down_total = jnp.zeros(expert_down.shape, jnp.float32)
    out_buffer = jnp.zeros(tokens_in.shape, jnp.bfloat16)
    grad_buffer = jnp.zeros(tokens_in.shape, jnp.bfloat16)
    slot_rows = jnp.arange(slots, dtype=jnp.int32)
    labels = jnp.arange(experts, dtype=jnp.int32)

    def expert_work(received):
        pre = jnp.einsum("sxcd,xdf->sxcf", received, expert_up, preferred_element_type=jnp.float32)
        hidden = jax.nn.gelu(pre, approximate=False).astype(jnp.bfloat16)
        produced = jnp.einsum(
            "sxcf,xfd->sxcd", hidden, expert_down, preferred_element_type=jnp.float32
        ).astype(jnp.bfloat16)
        return (produced, pre, received)

    def micro_step(index, carry):
        totals, up_total, down_total, out_buffer, grad_buffer = carry
        tokens = lax.dynamic_index_in_dim(tokens_in, index, 0, keepdims=False)[0]
        picks = lax.dynamic_index_in_dim(picks_in, index, 0, keepdims=False)[0]
        ranks = lax.dynamic_index_in_dim(ranks_in, index, 0, keepdims=False)[0]
        incoming = lax.dynamic_index_in_dim(cotangent, index, 0, keepdims=False)[0].astype(
            jnp.float32
        )
        weights = (
            lax.all_gather(first_gain, "fsdp", axis=0, tiled=True),
            lax.all_gather(first_shift, "fsdp", axis=0, tiled=True),
            lax.all_gather(attend_weight, "fsdp", axis=0, tiled=True),
            lax.all_gather(output_weight, "fsdp", axis=0, tiled=True),
            lax.all_gather(second_gain, "fsdp", axis=0, tiled=True),
            lax.all_gather(second_shift, "fsdp", axis=0, tiled=True),
            lax.all_gather(router_weight, "fsdp", axis=0, tiled=True),
        )
        gain_one = weights[0].astype(jnp.float32)
        shift_one = weights[1].astype(jnp.float32)
        gain_two = weights[4].astype(jnp.float32)
        shift_two = weights[5].astype(jnp.float32)
        attend, output, router = (weights[2], weights[3], weights[6])
        inputs = tokens.astype(jnp.float32)
        normed = layer_norm(inputs, gain_one, shift_one).astype(jnp.bfloat16)
        joined = jnp.dot(normed, attend, preferred_element_type=jnp.float32).astype(jnp.bfloat16)
        queries = joined[:, :width].reshape(length, HEADS, HEAD_DIM)
        keys = joined[:, width : 2 * width].reshape(length, HEADS, HEAD_DIM)
        values = joined[:, 2 * width :].reshape(length, HEADS, HEAD_DIM)
        scores = (
            jnp.einsum("qhd,khd->hqk", queries, keys, preferred_element_type=jnp.float32) * scale
        )
        highest = jnp.max(scores, axis=-1, keepdims=True)
        raised = jnp.exp(scores - highest)
        summed = jnp.sum(raised, axis=-1, keepdims=True)
        log_total = highest + jnp.log(summed)
        probs_low = (raised / summed).astype(jnp.bfloat16)
        mixed = (
            jnp.einsum("hqk,khd->qhd", probs_low, values, preferred_element_type=jnp.float32)
            .reshape(length, width)
            .astype(jnp.bfloat16)
        )
        middle = inputs + jnp.dot(mixed, output, preferred_element_type=jnp.float32)
        second = layer_norm(middle, gain_two, shift_two).astype(jnp.bfloat16)
        logits = jnp.dot(second, router, preferred_element_type=jnp.float32)
        gates = jax.nn.softmax(logits, axis=-1)
        slot, kept = route(picks, ranks, capacity)
        table = jnp.zeros((slots, length), jnp.float32)
        for choice_index in range(2):
            hit = (slot_rows[:, None] == slot[None, :, choice_index]) & kept[None, :, choice_index]
            table = table + jnp.where(hit, 1.0, 0.0)
        table = table.astype(jnp.bfloat16)
        outgoing = jnp.dot(table, second, preferred_element_type=jnp.float32).astype(jnp.bfloat16)
        outgoing = outgoing.reshape(groups, local_experts, CAP, width)
        pair_weights = []
        slot_grad = jnp.zeros((slots, width), jnp.float32)
        for choice_index in range(2):
            gate = jnp.sum(
                jnp.where(picks[:, choice_index, None] == labels[None, :], gates, 0.0), axis=1
            )
            pair_weight = jnp.where(kept[:, choice_index], gate, 0.0)
            pair_weights.append(pair_weight)
            slot_grad = slot_grad.at[slot[:, choice_index]].add(pair_weight[:, None] * incoming)
        sent = slot_grad.astype(jnp.bfloat16).reshape(groups, local_experts, CAP, width)
        produced, pre, received = expert_work(
            lax.all_to_all(outgoing, "fsdp", split_axis=0, concat_axis=0, tiled=True)
        )
        returned = (
            lax.all_to_all(produced, "fsdp", split_axis=0, concat_axis=0, tiled=True)
            .reshape(slots, width)
            .astype(jnp.float32)
        )
        result = middle
        gates_grad = jnp.zeros((length, experts), jnp.float32)
        for choice_index in range(2):
            fetched = jnp.take(returned, slot[:, choice_index], axis=0)
            result = result + pair_weights[choice_index][:, None] * fetched
            gate_grad = jnp.where(kept[:, choice_index], jnp.sum(incoming * fetched, axis=1), 0.0)
            gates_grad = gates_grad + jnp.where(
                picks[:, choice_index, None] == labels[None, :], gate_grad[:, None], 0.0
            )
        out_buffer = lax.dynamic_update_index_in_dim(
            out_buffer, result.astype(jnp.bfloat16)[None], index, 0
        )
        weights = (
            lax.all_gather(first_gain, "fsdp", axis=0, tiled=True),
            lax.all_gather(first_shift, "fsdp", axis=0, tiled=True),
            lax.all_gather(attend_weight, "fsdp", axis=0, tiled=True),
            lax.all_gather(output_weight, "fsdp", axis=0, tiled=True),
            lax.all_gather(second_gain, "fsdp", axis=0, tiled=True),
            lax.all_gather(second_shift, "fsdp", axis=0, tiled=True),
            lax.all_gather(router_weight, "fsdp", axis=0, tiled=True),
        )
        attend, output, router = (weights[2], weights[3], weights[6])
        logits_grad = (
            gates * (gates_grad - jnp.sum(gates * gates_grad, axis=1, keepdims=True))
        ).astype(jnp.bfloat16)
        router_grad = contract_rows(second, logits_grad)
        second_grad = contract_cols(logits_grad, router)
        arrived = lax.all_to_all(sent, "fsdp", split_axis=0, concat_axis=0, tiled=True)
        hidden = jax.nn.gelu(pre, approximate=False).astype(jnp.bfloat16)
        down_total = down_total + jnp.einsum(
            "sxcf,sxcd->xfd", hidden, arrived, preferred_element_type=jnp.float32
        )
        hidden_grad = jnp.einsum(
            "sxcd,xfd->sxcf", arrived, expert_down, preferred_element_type=jnp.float32
        )
        unused, gelu_pull = jax.vjp(lambda value: jax.nn.gelu(value, approximate=False), pre)
        pre_grad = gelu_pull(hidden_grad)[0].astype(jnp.bfloat16)
        up_total = up_total + jnp.einsum(
            "sxcd,sxcf->xdf", received, pre_grad, preferred_element_type=jnp.float32
        )
        rows_grad = jnp.einsum(
            "sxcf,xdf->sxcd", pre_grad, expert_up, preferred_element_type=jnp.float32
        ).astype(jnp.bfloat16)
        back = lax.all_to_all(rows_grad, "fsdp", split_axis=0, concat_axis=0, tiled=True).reshape(
            slots, width
        )
        second_grad = second_grad + contract_rows(table, back)
        unused_two, norm_pull = jax.vjp(layer_norm, middle, gain_two, shift_two)
        middle_part, gain_two_grad, shift_two_grad = norm_pull(second_grad)
        middle_grad = incoming + middle_part
        branch_grad = middle_grad.astype(jnp.bfloat16)
        output_grad = contract_rows(mixed, branch_grad)
        mixed_grad = (
            contract_cols(branch_grad, output).astype(jnp.bfloat16).reshape(length, HEADS, HEAD_DIM)
        )
        scores = (
            jnp.einsum("qhd,khd->hqk", queries, keys, preferred_element_type=jnp.float32) * scale
        )
        probs = jnp.exp(scores - log_total)
        values_grad = jnp.einsum(
            "hqk,qhd->khd",
            probs.astype(jnp.bfloat16),
            mixed_grad,
            preferred_element_type=jnp.float32,
        ).astype(jnp.bfloat16)
        probs_grad = jnp.einsum(
            "qhd,khd->hqk", mixed_grad, values, preferred_element_type=jnp.float32
        )
        delta = jnp.sum(probs * probs_grad, axis=-1, keepdims=True)
        scores_grad = (probs * (probs_grad - delta)).astype(jnp.bfloat16)
        queries_grad = (
            jnp.einsum("hqk,khd->qhd", scores_grad, keys, preferred_element_type=jnp.float32)
            * scale
        ).astype(jnp.bfloat16)
        keys_grad = (
            jnp.einsum("hqk,qhd->khd", scores_grad, queries, preferred_element_type=jnp.float32)
            * scale
        ).astype(jnp.bfloat16)
        joined_grad = jnp.concatenate(
            [
                queries_grad.reshape(length, width),
                keys_grad.reshape(length, width),
                values_grad.reshape(length, width),
            ],
            axis=1,
        )
        attend_grad = contract_rows(normed, joined_grad)
        normed_grad = contract_cols(joined_grad, attend)
        unused_three, first_pull = jax.vjp(layer_norm, inputs, gain_one, shift_one)
        inputs_part, gain_one_grad, shift_one_grad = first_pull(normed_grad)
        tokens_grad = (middle_grad + inputs_part).astype(jnp.bfloat16)
        grad_buffer = lax.dynamic_update_index_in_dim(grad_buffer, tokens_grad[None], index, 0)
        added = (
            gain_one_grad,
            shift_one_grad,
            attend_grad,
            output_grad,
            gain_two_grad,
            shift_two_grad,
            router_grad,
        )
        totals = tuple((left + right for left, right in zip(totals, added)))
        return (totals, up_total, down_total, out_buffer, grad_buffer)

    totals, up_total, down_total, out_buffer, grad_buffer = lax.fori_loop(
        0, micro, micro_step, (totals, up_total, down_total, out_buffer, grad_buffer)
    )
    shards = (
        lax.psum_scatter(
            totals[0].astype(jnp.bfloat16), "fsdp", scatter_dimension=0, tiled=True
        ).astype(jnp.float32),
        lax.psum_scatter(
            totals[1].astype(jnp.bfloat16), "fsdp", scatter_dimension=0, tiled=True
        ).astype(jnp.float32),
        lax.psum_scatter(
            totals[2].astype(jnp.bfloat16), "fsdp", scatter_dimension=0, tiled=True
        ).astype(jnp.float32),
        lax.psum_scatter(
            totals[3].astype(jnp.bfloat16), "fsdp", scatter_dimension=0, tiled=True
        ).astype(jnp.float32),
        lax.psum_scatter(
            totals[4].astype(jnp.bfloat16), "fsdp", scatter_dimension=0, tiled=True
        ).astype(jnp.float32),
        lax.psum_scatter(
            totals[5].astype(jnp.bfloat16), "fsdp", scatter_dimension=0, tiled=True
        ).astype(jnp.float32),
        lax.psum_scatter(
            totals[6].astype(jnp.bfloat16), "fsdp", scatter_dimension=0, tiled=True
        ).astype(jnp.float32),
    )
    summed = lax.psum(
        (
            shards[0],
            shards[1],
            shards[2],
            shards[3],
            shards[4],
            shards[5],
            shards[6],
            up_total,
            down_total,
        ),
        "replica",
    )
    return (
        out_buffer,
        grad_buffer,
        summed[0],
        summed[1],
        summed[2],
        summed[3],
        summed[4],
        summed[5],
        summed[6],
        summed[7],
        summed[8],
    )


def solution(mesh):
    in_specs = (
        P(None, ("replica", "fsdp"), None, None),
        P(None, ("replica", "fsdp"), None, None),
        P(None, ("replica", "fsdp"), None),
        P(),
        P("fsdp"),
        P("fsdp"),
        P("fsdp", None),
        P("fsdp", None),
        P("fsdp"),
        P("fsdp"),
        P("fsdp", None),
        P("fsdp", None, None),
        P("fsdp", None, None),
        P(None, ("replica", "fsdp"), None, None),
    )
    out_specs = (
        P(None, ("replica", "fsdp"), None, None),
        P(None, ("replica", "fsdp"), None, None),
        P("fsdp"),
        P("fsdp"),
        P("fsdp", None),
        P("fsdp", None),
        P("fsdp"),
        P("fsdp"),
        P("fsdp", None),
        P("fsdp", None, None),
        P("fsdp", None, None),
    )
    return jax.shard_map(body, mesh=mesh, in_specs=in_specs, out_specs=out_specs, check_vma=False)
```

profile of v0, /device:TPU:0, one launch (start us, length us, event | category | flops | bytes accessed | tf_op | source)
XLA Modules:
  0.0 1119.1 jit_solution(11041064828713295726)
XLA Ops:
  12.1 857.8 %while.35 = (s32[]{:T(128)}, f32[384]{0:T(512)}, f32[384]{0:T(512)}, f32[384,1152]{1,0:T(8,128)}, f32[384,384]{1,0:T(8,128)}, /*index=5*/f32[384]{0:T(512)}, f32...) while((s32[]{:T(128)}, f32[384]{0:T(512)}, ...), condition=%wide.region_27.29_spmd.clone.clone, body=%wide.region_0.28_spmd.clone.clone.sunk | while | flops 4755731456 | bytes 166873360 | solution.py:275
  20.4 34.9 %all-reduce.20 = (bf16[384]{0:T(512)(128)(2,1)S(1)}, bf16[384]{0:T(512)(128)(2,1)S(1)}, bf16[384]{0:T(512)(128)(2,1)S(1)}, bf16[384]{0:T(512)(128)(2,1)S(1)}) all-reduce(bf16[384]{0:T(512)(128)(2,1)S(1)} %dynamic-update-slice.12, bf16[384]{0:T(512)(128)(2,1)S(1)} %dynamic-update-slice.13, ...), channel_id=1, replica_groups=mesh['replica'=2,'fsdp'=16] {'fsdp'}, use_global_device_ids=true, to_apply=%add.1 | all-reduce | flops 1536 | bytes 6144 | tf_op jit(solution)/shard_map/while
  58.1 18.2 %all_gather.66 = bf16[384,384]{1,0:T(8,128)(2,1)S(1)} all-gather(bf16[24,384]{1,0:T(8,128)(2,1)} %get-tuple-element.1270), channel_id=1, replica_groups=mesh['replica'=2,'fsdp'=16] {'fsdp'}, dimensions={0}, use_global_device_ids=true | all-gather | bytes 313344 | tf_op jit(solution)/shard_map/while/body/eval_jaxpr/all_gather | solution.py:112
  76.3 21.9 %all_gather.65 = bf16[384,1152]{1,0:T(8,128)(2,1)S(1)} all-gather(bf16[24,1152]{1,0:T(8,128)(2,1)} %get-tuple-element.1268), channel_id=1, replica_groups=mesh['replica'=2,'fsdp'=16] {'fsdp'}, dimensions={0}, use_global_device_ids=true | all-gather | bytes 940032 | tf_op jit(solution)/shard_map/while/body/eval_jaxpr/all_gather | solution.py:111
  104.4 3.6 all-to-all-start
  108.0 23.0 %all_gather.67 = bf16[384,32]{1,0:T(8,128)(2,1)S(1)} all-gather(bf16[24,32]{1,0:T(8,128)(2,1)S(1)} %copy-done.46), channel_id=1, replica_groups=mesh['replica'=2,'fsdp'=16] {'fsdp'}, dimensions={0}, use_global_device_ids=true | all-gather | bytes 26112 | tf_op jit(solution)/shard_map/while/body/eval_jaxpr/all_gather | solution.py:115
  132.2 10.3 fusion.265
  144.5 4.2 all-to-all-start.1
  150.6 10.3 all-to-all-done.1
  175.2 3.6 all-to-all-start.2
  184.9 6.0 all-to-all-done.2
  190.9 5.3 fusion.270
  198.2 4.2 all-to-all-start.3
  202.5 4.6 bitcast_add_fusion.4
  210.4 4.3 all-to-all-done.3
  236.5 31.5 %all-reduce.20 = (bf16[384]{0:T(512)(128)(2,1)S(1)}, bf16[384]{0:T(512)(128)(2,1)S(1)}, bf16[384]{0:T(512)(128)(2,1)S(1)}, bf16[384]{0:T(512)(128)(2,1)S(1)}) all-reduce(bf16[384]{0:T(512)(128)(2,1)S(1)} %dynamic-update-slice.12, bf16[384]{0:T(512)(128)(2,1)S(1)} %dynamic-update-slice.13, ...), channel_id=1, replica_groups=mesh['replica'=2,'fsdp'=16] {'fsdp'}, use_global_device_ids=true, to_apply=%add.1 | all-reduce | flops 1536 | bytes 6144 | tf_op jit(solution)/shard_map/while
  270.8 18.2 %all_gather.66 = bf16[384,384]{1,0:T(8,128)(2,1)S(1)} all-gather(bf16[24,384]{1,0:T(8,128)(2,1)} %get-tuple-element.1270), channel_id=1, replica_groups=mesh['replica'=2,'fsdp'=16] {'fsdp'}, dimensions={0}, use_global_device_ids=true | all-gather | bytes 313344 | tf_op jit(solution)/shard_map/while/body/eval_jaxpr/all_gather | solution.py:112
  289.0 21.8 %all_gather.65 = bf16[384,1152]{1,0:T(8,128)(2,1)S(1)} all-gather(bf16[24,1152]{1,0:T(8,128)(2,1)} %get-tuple-element.1268), channel_id=1, replica_groups=mesh['replica'=2,'fsdp'=16] {'fsdp'}, dimensions={0}, use_global_device_ids=true | all-gather | bytes 940032 | tf_op jit(solution)/shard_map/while/body/eval_jaxpr/all_gather | solution.py:111
  317.0 3.6 all-to-all-start
  320.5 23.0 %all_gather.67 = bf16[384,32]{1,0:T(8,128)(2,1)S(1)} all-gather(bf16[24,32]{1,0:T(8,128)(2,1)S(1)} %copy-done.46), channel_id=1, replica_groups=mesh['replica'=2,'fsdp'=16] {'fsdp'}, dimensions={0}, use_global_device_ids=true | all-gather | bytes 26112 | tf_op jit(solution)/shard_map/while/body/eval_jaxpr/all_gather | solution.py:115
  344.8 10.3 fusion.265
  357.1 4.2 all-to-all-start.1
  363.2 10.3 all-to-all-done.1
  387.8 3.6 all-to-all-start.2
  397.5 6.0 all-to-all-done.2
  403.5 5.3 fusion.270
  410.8 4.2 all-to-all-start.3
  415.0 6.0 bitcast_add_fusion.4
  421.1 5.7 bitcast_add_fusion.5
  449.1 33.3 %all-reduce.20 = (bf16[384]{0:T(512)(128)(2,1)S(1)}, bf16[384]{0:T(512)(128)(2,1)S(1)}, bf16[384]{0:T(512)(128)(2,1)S(1)}, bf16[384]{0:T(512)(128)(2,1)S(1)}) all-reduce(bf16[384]{0:T(512)(128)(2,1)S(1)} %dynamic-update-slice.12, bf16[384]{0:T(512)(128)(2,1)S(1)} %dynamic-update-slice.13, ...), channel_id=1, replica_groups=mesh['replica'=2,'fsdp'=16] {'fsdp'}, use_global_device_ids=true, to_apply=%add.1 | all-reduce | flops 1536 | bytes 6144 | tf_op jit(solution)/shard_map/while
  485.3 18.2 %all_gather.66 = bf16[384,384]{1,0:T(8,128)(2,1)S(1)} all-gather(bf16[24,384]{1,0:T(8,128)(2,1)} %get-tuple-element.1270), channel_id=1, replica_groups=mesh['replica'=2,'fsdp'=16] {'fsdp'}, dimensions={0}, use_global_device_ids=true | all-gather | bytes 313344 | tf_op jit(solution)/shard_map/while/body/eval_jaxpr/all_gather | solution.py:112
  503.5 21.9 %all_gather.65 = bf16[384,1152]{1,0:T(8,128)(2,1)S(1)} all-gather(bf16[24,1152]{1,0:T(8,128)(2,1)} %get-tuple-element.1268), channel_id=1, replica_groups=mesh['replica'=2,'fsdp'=16] {'fsdp'}, dimensions={0}, use_global_device_ids=true | all-gather | bytes 940032 | tf_op jit(solution)/shard_map/while/body/eval_jaxpr/all_gather | solution.py:111
  531.5 3.6 all-to-all-start
  535.1 23.0 %all_gather.67 = bf16[384,32]{1,0:T(8,128)(2,1)S(1)} all-gather(bf16[24,32]{1,0:T(8,128)(2,1)S(1)} %copy-done.46), channel_id=1, replica_groups=mesh['replica'=2,'fsdp'=16] {'fsdp'}, dimensions={0}, use_global_device_ids=true | all-gather | bytes 26112 | tf_op jit(solution)/shard_map/while/body/eval_jaxpr/all_gather | solution.py:115
  559.4 10.3 fusion.265
  571.7 4.2 all-to-all-start.1
  577.8 10.3 all-to-all-done.1
  602.3 3.6 all-to-all-start.2
  612.1 6.0 all-to-all-done.2
  618.1 5.3 fusion.270
  625.4 4.2 all-to-all-start.3
  629.6 6.0 bitcast_add_fusion.4
  635.6 5.7 bitcast_add_fusion.5
  663.7 33.3 %all-reduce.20 = (bf16[384]{0:T(512)(128)(2,1)S(1)}, bf16[384]{0:T(512)(128)(2,1)S(1)}, bf16[384]{0:T(512)(128)(2,1)S(1)}, bf16[384]{0:T(512)(128)(2,1)S(1)}) all-reduce(bf16[384]{0:T(512)(128)(2,1)S(1)} %dynamic-update-slice.12, bf16[384]{0:T(512)(128)(2,1)S(1)} %dynamic-update-slice.13, ...), channel_id=1, replica_groups=mesh['replica'=2,'fsdp'=16] {'fsdp'}, use_global_device_ids=true, to_apply=%add.1 | all-reduce | flops 1536 | bytes 6144 | tf_op jit(solution)/shard_map/while
  699.8 18.2 %all_gather.66 = bf16[384,384]{1,0:T(8,128)(2,1)S(1)} all-gather(bf16[24,384]{1,0:T(8,128)(2,1)} %get-tuple-element.1270), channel_id=1, replica_groups=mesh['replica'=2,'fsdp'=16] {'fsdp'}, dimensions={0}, use_global_device_ids=true | all-gather | bytes 313344 | tf_op jit(solution)/shard_map/while/body/eval_jaxpr/all_gather | solution.py:112
  718.0 21.9 %all_gather.65 = bf16[384,1152]{1,0:T(8,128)(2,1)S(1)} all-gather(bf16[24,1152]{1,0:T(8,128)(2,1)} %get-tuple-element.1268), channel_id=1, replica_groups=mesh['replica'=2,'fsdp'=16] {'fsdp'}, dimensions={0}, use_global_device_ids=true | all-gather | bytes 940032 | tf_op jit(solution)/shard_map/while/body/eval_jaxpr/all_gather | solution.py:111
  746.1 3.6 all-to-all-start
  749.7 23.0 %all_gather.67 = bf16[384,32]{1,0:T(8,128)(2,1)S(1)} all-gather(bf16[24,32]{1,0:T(8,128)(2,1)S(1)} %copy-done.46), channel_id=1, replica_groups=mesh['replica'=2,'fsdp'=16] {'fsdp'}, dimensions={0}, use_global_device_ids=true | all-gather | bytes 26112 | tf_op jit(solution)/shard_map/while/body/eval_jaxpr/all_gather | solution.py:115
  773.9 10.3 fusion.265
  786.2 4.2 all-to-all-start.1
  792.3 10.3 all-to-all-done.1
  816.9 3.6 all-to-all-start.2
  826.6 6.0 all-to-all-done.2
  832.6 5.3 fusion.270
  839.9 4.2 all-to-all-start.3
  844.2 6.0 bitcast_add_fusion.4
  850.2 5.7 bitcast_add_fusion.5
  880.1 33.4 %all-reduce.18 = (bf16[384]{0:T(512)(128)(2,1)S(1)}, bf16[384]{0:T(512)(128)(2,1)S(1)}, bf16[384]{0:T(512)(128)(2,1)S(1)}, bf16[384]{0:T(512)(128)(2,1)S(1)}) all-reduce(bf16[384]{0:T(512)(128)(2,1)S(1)} %convert_element_type.283, ...), channel_id=2, replica_groups=mesh['replica'=2,'fsdp'=16] {'fsdp'}, use_global_device_ids=true, to_apply=%region_28.30.clone | all-reduce | flops 1536 | bytes 6144
  913.6 12.1 %reduce-scatter.14.cloned.1.call-done = bf16[24,32]{1,0:T(8,128)(2,1)} async-done(((bf16[384,32]{1,0:T(8,128)(2,1)}), bf16[24,32]{1,0:T(8,128)(2,1)}) %reduce-scatter.14.cloned.1.call-update) | async-done | bytes 1552
  925.7 56.9 %reduce-scatter.12.cloned.1.call-done = bf16[24,384]{1,0:T(8,128)(2,1)} async-done(((bf16[384,384]{1,0:T(8,128)(2,1)}), bf16[24,384]{1,0:T(8,128)(2,1)}) %reduce-scatter.12.cloned.1.call-update) | async-done | bytes 18448
  982.6 58.7 %reduce-scatter.10.cloned.1.call-done = bf16[24,1152]{1,0:T(8,128)(2,1)} async-done(((bf16[384,1152]{1,0:T(8,128)(2,1)}), bf16[24,1152]{1,0:T(8,128)(2,1)}) %reduce-scatter.10.cloned.1.call-update) | async-done | bytes 55312
  1041.3 15.1 %all-reduce.25 = (f32[24]{0:T(128)}, f32[24]{0:T(128)}, f32[24,1152]{1,0:T(8,128)}, f32[24,384]{1,0:T(8,128)}, f32[24]{0:T(128)}, /*index=5*/f32[24]{0:T(128)}, f32[24,32]{1,0:T(8,128)}) all-reduce(f32[24]{0:T(128)S(1)} %get-tuple-element.929, f32[24]{0:T(128)S(1)} %get-tuple-element.928, ...), channel_id=1, replica_groups=mesh['replica'=2,'fsdp'=16] {'replica'}, use_global_device_ids=true, to_apply=%region_29.31 | all-reduce | flops 37728 | bytes 226560 | tf_op jit(solution)/shard_map/psum | solution.py:301
  1056.3 48.4 %all-reduce.24.cloned.1.call-done = (f32[2,384,1536]{2,1,0:T(8,128)}, f32[2,1536,384]{2,1,0:T(8,128)}) async-done(((f32[2,384,1536]{2,1,0:T(8,128)}, f32[2,1536,384]{2,1,0:T(8,128)}), (f32[2,384,1536]{2,1,0:T(8,128)}, f32[2,1536,384]{2,1,0:T(8,128)})) %all-reduce.24.cloned.1.call-update) | async-done | bytes 9437200 | tf_op jit(solution)/shard_map/psum | solution.py:301
  1104.7 5.0 copy.217
  (962 shorter events, 247.9 us)
Async XLA Ops:
  8.0 917.7 %reduce-scatter.14.cloned.1.call-start = ((), (), s32[]{:S(2)}) async-start(), calls=%async_computation.9 | async-start | bytes 104448
  13.9 84.3 %copy-start.22 = (f32[197]{0:T(256)}, f32[197]{0:T(256)S(1)}, u32[]{:S(2)}) copy-start(f32[197]{0:T(256)S(1)} %broadcast_multiply_fusion.4) | copy-start | bytes 2368 | tf_op jit(solution)/shard_map/while
  15.0 83.2 %copy-start.27 = (f32[197]{0:T(256)}, f32[197]{0:T(256)S(1)}, u32[]{:S(2)}) copy-start(f32[197]{0:T(256)S(1)} %fusion.256) | copy-start | bytes 2368 | tf_op jit(solution)/shard_map/while
  55.3 42.9 %copy-start.19 = (f32[384]{0:T(512)}, f32[384]{0:T(512)S(1)}, u32[]{:S(2)}) copy-start(f32[384]{0:T(512)S(1)} %convert_element_type.530) | copy-start | bytes 4612 | tf_op jit(solution)/shard_map/while
  55.3 47.7 %copy-start.33 = (f32[384]{0:T(512)}, f32[384]{0:T(512)S(1)}, u32[]{:S(2)}) copy-start(f32[384]{0:T(512)S(1)} %convert_element_type.532) | copy-start | bytes 4612 | tf_op jit(solution)/shard_map/while
  55.3 42.9 %copy-start.31 = (f32[384]{0:T(512)}, f32[384]{0:T(512)S(1)}, u32[]{:S(2)}) copy-start(f32[384]{0:T(512)S(1)} %convert_element_type.531) | copy-start | bytes 4612 | tf_op jit(solution)/shard_map/while
  56.1 42.2 %copy-start.25 = (s32[197,1]{0,1:T(1,128)}, s32[197,1]{0,1:T(1,128)S(1)}, u32[]{:S(2)}) copy-start(s32[197,1]{0,1:T(1,128)S(1)} %get-tuple-element.1151) | copy-start | bytes 2368 | tf_op jit(solution)/shard_map/while
  56.1 42.2 %copy-start.26 = (s32[197,1]{0,1:T(1,128)}, s32[197,1]{0,1:T(1,128)S(1)}, u32[]{:S(2)}) copy-start(s32[197,1]{0,1:T(1,128)S(1)} %get-tuple-element.1147) | copy-start | bytes 2368 | tf_op jit(solution)/shard_map/while
  57.5 45.7 %copy-start.63 = (pred[197]{0:T(512)(128)(4,1)}, pred[197]{0:T(512)(128)(4,1)S(1)}, u32[]{:S(2)}) copy-start(pred[197]{0:T(512)(128)(4,1)S(1)} %get-tuple-element.1155) | copy-start | bytes 595 | tf_op jit(solution)/shard_map/while
  57.5 45.7 %copy-start.65 = (pred[197]{0:T(512)(128)(4,1)}, pred[197]{0:T(512)(128)(4,1)S(1)}, u32[]{:S(2)}) copy-start(pred[197]{0:T(512)(128)(4,1)S(1)} %get-tuple-element.1154) | copy-start | bytes 595 | tf_op jit(solution)/shard_map/while
  58.1 91.5 %copy-start.49 = (s32[197,1]{0,1:T(1,128)}, s32[197,1]{0,1:T(1,128)S(1)}, u32[]{:S(2)}) copy-start(s32[197,1]{0,1:T(1,128)S(1)} %get-tuple-element.1153) | copy-start | bytes 2368 | tf_op jit(solution)/shard_map/while
  58.1 92.0 %copy-start.47 = (s32[197,1]{0,1:T(1,128)}, s32[197,1]{0,1:T(1,128)S(1)}, u32[]{:S(2)}) copy-start(s32[197,1]{0,1:T(1,128)S(1)} %get-tuple-element.1152) | copy-start | bytes 2368 | tf_op jit(solution)/shard_map/while
  103.2 45.6 %copy-start.15 = (bf16[197,384]{1,0:T(8,128)(2,1)}, bf16[197,384]{1,0:T(8,128)(2,1)S(1)}, u32[]{:S(2)}) copy-start(bf16[197,384]{1,0:T(8,128)(2,1)S(1)} %add_convert_fusion.9) | copy-start | bytes 453892 | tf_op jit(solution)/shard_map/while
  104.4 27.8 %all-to-all-start = ((bf16[16,2,16,384]{3,2,1,0:T(8,128)(2,1)}), bf16[16,2,16,384]{3,2,1,0:T(8,128)(2,1)S(1)}, u32[]{:S(2)}, u32[]{:S(2)}) async-start(bf16[16,2,16,384]{3,2,1,0:T(8,128)(2,1)} %bitcast.391), calls=%async_computation | async-start | bytes 786432 | tf_op jit(solution)/shard_map/while/body/eval_jaxpr/all_to_all | solution.py:164
  144.5 16.4 %all-to-all-start.1 = ((bf16[16,2,16,384]{3,2,1,0:T(8,128)(2,1)}), bf16[16,2,16,384]{3,2,1,0:T(8,128)(2,1)}, u32[]{:S(2)}, u32[]{:S(2)}) async-start(bf16[16,2,16,384]{3,2,1,0:T(8,128)(2,1)} %copy.159), calls=%async_computation.1 | async-start | bytes 786432 | tf_op jit(solution)/shard_map/while/body/eval_jaxpr/all_to_all | solution.py:167
  175.2 15.7 %all-to-all-start.2 = ((bf16[16,2,16,384]{3,2,1,0:T(8,128)(2,1)}), bf16[16,2,16,384]{3,2,1,0:T(8,128)(2,1)S(1)}, u32[]{:S(2)}, u32[]{:S(2)}) async-start(bf16[16,2,16,384]{3,2,1,0:T(8,128)(2,1)} %bitcast.414), calls=%async_computation.2 | async-start | bytes 786432 | tf_op jit(solution)/shard_map/while/body/eval_jaxpr/all_to_all | solution.py:198
  198.2 16.4 %all-to-all-start.3 = ((bf16[16,2,16,384]{3,2,1,0:T(8,128)(2,1)}), bf16[16,2,16,384]{3,2,1,0:T(8,128)(2,1)}, u32[]{:S(2)}, u32[]{:S(2)}) async-start(bf16[16,2,16,384]{3,2,1,0:T(8,128)(2,1)} %copy.160), calls=%async_computation.3 | async-start | bytes 786432 | tf_op jit(solution)/shard_map/while/body/eval_jaxpr/all_to_all | solution.py:214
  230.0 80.8 %copy-start.22 = (f32[197]{0:T(256)}, f32[197]{0:T(256)S(1)}, u32[]{:S(2)}) copy-start(f32[197]{0:T(256)S(1)} %broadcast_multiply_fusion.4) | copy-start | bytes 2368 | tf_op jit(solution)/shard_map/while
  231.2 79.6 %copy-start.27 = (f32[197]{0:T(256)}, f32[197]{0:T(256)S(1)}, u32[]{:S(2)}) copy-start(f32[197]{0:T(256)S(1)} %fusion.256) | copy-start | bytes 2368 | tf_op jit(solution)/shard_map/while
  268.0 42.8 %copy-start.19 = (f32[384]{0:T(512)}, f32[384]{0:T(512)S(1)}, u32[]{:S(2)}) copy-start(f32[384]{0:T(512)S(1)} %convert_element_type.530) | copy-start | bytes 4612 | tf_op jit(solution)/shard_map/while
  268.0 47.6 %copy-start.33 = (f32[384]{0:T(512)}, f32[384]{0:T(512)S(1)}, u32[]{:S(2)}) copy-start(f32[384]{0:T(512)S(1)} %convert_element_type.532) | copy-start | bytes 4612 | tf_op jit(solution)/shard_map/while
  268.0 42.8 %copy-start.31 = (f32[384]{0:T(512)}, f32[384]{0:T(512)S(1)}, u32[]{:S(2)}) copy-start(f32[384]{0:T(512)S(1)} %convert_element_type.531) | copy-start | bytes 4612 | tf_op jit(solution)/shard_map/while
  270.2 45.6 %copy-start.63 = (pred[197]{0:T(512)(128)(4,1)}, pred[197]{0:T(512)(128)(4,1)S(1)}, u32[]{:S(2)}) copy-start(pred[197]{0:T(512)(128)(4,1)S(1)} %get-tuple-element.1155) | copy-start | bytes 595 | tf_op jit(solution)/shard_map/while
  270.2 45.6 %copy-start.65 = (pred[197]{0:T(512)(128)(4,1)}, pred[197]{0:T(512)(128)(4,1)S(1)}, u32[]{:S(2)}) copy-start(pred[197]{0:T(512)(128)(4,1)S(1)} %get-tuple-element.1154) | copy-start | bytes 595 | tf_op jit(solution)/shard_map/while
  270.8 91.4 %copy-start.49 = (s32[197,1]{0,1:T(1,128)}, s32[197,1]{0,1:T(1,128)S(1)}, u32[]{:S(2)}) copy-start(s32[197,1]{0,1:T(1,128)S(1)} %get-tuple-element.1153) | copy-start | bytes 2368 | tf_op jit(solution)/shard_map/while
  270.8 91.9 %copy-start.47 = (s32[197,1]{0,1:T(1,128)}, s32[197,1]{0,1:T(1,128)S(1)}, u32[]{:S(2)}) copy-start(s32[197,1]{0,1:T(1,128)S(1)} %get-tuple-element.1152) | copy-start | bytes 2368 | tf_op jit(solution)/shard_map/while
  315.8 45.6 %copy-start.15 = (bf16[197,384]{1,0:T(8,128)(2,1)}, bf16[197,384]{1,0:T(8,128)(2,1)S(1)}, u32[]{:S(2)}) copy-start(bf16[197,384]{1,0:T(8,128)(2,1)S(1)} %add_convert_fusion.9) | copy-start | bytes 453892 | tf_op jit(solution)/shard_map/while
  317.0 27.8 %all-to-all-start = ((bf16[16,2,16,384]{3,2,1,0:T(8,128)(2,1)}), bf16[16,2,16,384]{3,2,1,0:T(8,128)(2,1)S(1)}, u32[]{:S(2)}, u32[]{:S(2)}) async-start(bf16[16,2,16,384]{3,2,1,0:T(8,128)(2,1)} %bitcast.391), calls=%async_computation | async-start | bytes 786432 | tf_op jit(solution)/shard_map/while/body/eval_jaxpr/all_to_all | solution.py:164
  357.1 16.4 %all-to-all-start.1 = ((bf16[16,2,16,384]{3,2,1,0:T(8,128)(2,1)}), bf16[16,2,16,384]{3,2,1,0:T(8,128)(2,1)}, u32[]{:S(2)}, u32[]{:S(2)}) async-start(bf16[16,2,16,384]{3,2,1,0:T(8,128)(2,1)} %copy.159), calls=%async_computation.1 | async-start | bytes 786432 | tf_op jit(solution)/shard_map/while/body/eval_jaxpr/all_to_all | solution.py:167
  387.8 15.7 %all-to-all-start.2 = ((bf16[16,2,16,384]{3,2,1,0:T(8,128)(2,1)}), bf16[16,2,16,384]{3,2,1,0:T(8,128)(2,1)S(1)}, u32[]{:S(2)}, u32[]{:S(2)}) async-start(bf16[16,2,16,384]{3,2,1,0:T(8,128)(2,1)} %bitcast.414), calls=%async_computation.2 | async-start | bytes 786432 | tf_op jit(solution)/shard_map/while/body/eval_jaxpr/all_to_all | solution.py:198
  410.8 16.4 %all-to-all-start.3 = ((bf16[16,2,16,384]{3,2,1,0:T(8,128)(2,1)}), bf16[16,2,16,384]{3,2,1,0:T(8,128)(2,1)}, u32[]{:S(2)}, u32[]{:S(2)}) async-start(bf16[16,2,16,384]{3,2,1,0:T(8,128)(2,1)} %copy.160), calls=%async_computation.3 | async-start | bytes 786432 | tf_op jit(solution)/shard_map/while/body/eval_jaxpr/all_to_all | solution.py:214
  442.6 82.7 %copy-start.22 = (f32[197]{0:T(256)}, f32[197]{0:T(256)S(1)}, u32[]{:S(2)}) copy-start(f32[197]{0:T(256)S(1)} %broadcast_multiply_fusion.4) | copy-start | bytes 2368 | tf_op jit(solution)/shard_map/while
  443.8 81.6 %copy-start.27 = (f32[197]{0:T(256)}, f32[197]{0:T(256)S(1)}, u32[]{:S(2)}) copy-start(f32[197]{0:T(256)S(1)} %fusion.256) | copy-start | bytes 2368 | tf_op jit(solution)/shard_map/while
  482.5 42.9 %copy-start.19 = (f32[384]{0:T(512)}, f32[384]{0:T(512)S(1)}, u32[]{:S(2)}) copy-start(f32[384]{0:T(512)S(1)} %convert_element_type.530) | copy-start | bytes 4612 | tf_op jit(solution)/shard_map/while
  482.5 47.7 %copy-start.33 = (f32[384]{0:T(512)}, f32[384]{0:T(512)S(1)}, u32[]{:S(2)}) copy-start(f32[384]{0:T(512)S(1)} %convert_element_type.532) | copy-start | bytes 4612 | tf_op jit(solution)/shard_map/while
  482.5 42.9 %copy-start.31 = (f32[384]{0:T(512)}, f32[384]{0:T(512)S(1)}, u32[]{:S(2)}) copy-start(f32[384]{0:T(512)S(1)} %convert_element_type.531) | copy-start | bytes 4612 | tf_op jit(solution)/shard_map/while
  483.2 42.2 %copy-start.26 = (s32[197,1]{0,1:T(1,128)}, s32[197,1]{0,1:T(1,128)S(1)}, u32[]{:S(2)}) copy-start(s32[197,1]{0,1:T(1,128)S(1)} %get-tuple-element.1147) | copy-start | bytes 2368 | tf_op jit(solution)/shard_map/while
  484.6 45.7 %copy-start.63 = (pred[197]{0:T(512)(128)(4,1)}, pred[197]{0:T(512)(128)(4,1)S(1)}, u32[]{:S(2)}) copy-start(pred[197]{0:T(512)(128)(4,1)S(1)} %get-tuple-element.1155) | copy-start | bytes 595 | tf_op jit(solution)/shard_map/while
  484.7 45.7 %copy-start.65 = (pred[197]{0:T(512)(128)(4,1)}, pred[197]{0:T(512)(128)(4,1)S(1)}, u32[]{:S(2)}) copy-start(pred[197]{0:T(512)(128)(4,1)S(1)} %get-tuple-element.1154) | copy-start | bytes 595 | tf_op jit(solution)/shard_map/while
  485.3 91.5 %copy-start.49 = (s32[197,1]{0,1:T(1,128)}, s32[197,1]{0,1:T(1,128)S(1)}, u32[]{:S(2)}) copy-start(s32[197,1]{0,1:T(1,128)S(1)} %get-tuple-element.1153) | copy-start | bytes 2368 | tf_op jit(solution)/shard_map/while
  485.3 92.0 %copy-start.47 = (s32[197,1]{0,1:T(1,128)}, s32[197,1]{0,1:T(1,128)S(1)}, u32[]{:S(2)}) copy-start(s32[197,1]{0,1:T(1,128)S(1)} %get-tuple-element.1152) | copy-start | bytes 2368 | tf_op jit(solution)/shard_map/while
  530.3 45.6 %copy-start.15 = (bf16[197,384]{1,0:T(8,128)(2,1)}, bf16[197,384]{1,0:T(8,128)(2,1)S(1)}, u32[]{:S(2)}) copy-start(bf16[197,384]{1,0:T(8,128)(2,1)S(1)} %add_convert_fusion.9) | copy-start | bytes 453892 | tf_op jit(solution)/shard_map/while
  531.5 27.8 %all-to-all-start = ((bf16[16,2,16,384]{3,2,1,0:T(8,128)(2,1)}), bf16[16,2,16,384]{3,2,1,0:T(8,128)(2,1)S(1)}, u32[]{:S(2)}, u32[]{:S(2)}) async-start(bf16[16,2,16,384]{3,2,1,0:T(8,128)(2,1)} %bitcast.391), calls=%async_computation | async-start | bytes 786432 | tf_op jit(solution)/shard_map/while/body/eval_jaxpr/all_to_all | solution.py:164
  571.7 16.4 %all-to-all-start.1 = ((bf16[16,2,16,384]{3,2,1,0:T(8,128)(2,1)}), bf16[16,2,16,384]{3,2,1,0:T(8,128)(2,1)}, u32[]{:S(2)}, u32[]{:S(2)}) async-start(bf16[16,2,16,384]{3,2,1,0:T(8,128)(2,1)} %copy.159), calls=%async_computation.1 | async-start | bytes 786432 | tf_op jit(solution)/shard_map/while/body/eval_jaxpr/all_to_all | solution.py:167
  602.3 15.7 %all-to-all-start.2 = ((bf16[16,2,16,384]{3,2,1,0:T(8,128)(2,1)}), bf16[16,2,16,384]{3,2,1,0:T(8,128)(2,1)S(1)}, u32[]{:S(2)}, u32[]{:S(2)}) async-start(bf16[16,2,16,384]{3,2,1,0:T(8,128)(2,1)} %bitcast.414), calls=%async_computation.2 | async-start | bytes 786432 | tf_op jit(solution)/shard_map/while/body/eval_jaxpr/all_to_all | solution.py:198
  625.4 16.4 %all-to-all-start.3 = ((bf16[16,2,16,384]{3,2,1,0:T(8,128)(2,1)}), bf16[16,2,16,384]{3,2,1,0:T(8,128)(2,1)}, u32[]{:S(2)}, u32[]{:S(2)}) async-start(bf16[16,2,16,384]{3,2,1,0:T(8,128)(2,1)} %copy.160), calls=%async_computation.3 | async-start | bytes 786432 | tf_op jit(solution)/shard_map/while/body/eval_jaxpr/all_to_all | solution.py:214
  657.2 82.7 %copy-start.22 = (f32[197]{0:T(256)}, f32[197]{0:T(256)S(1)}, u32[]{:S(2)}) copy-start(f32[197]{0:T(256)S(1)} %broadcast_multiply_fusion.4) | copy-start | bytes 2368 | tf_op jit(solution)/shard_map/while
  658.3 81.6 %copy-start.27 = (f32[197]{0:T(256)}, f32[197]{0:T(256)S(1)}, u32[]{:S(2)}) copy-start(f32[197]{0:T(256)S(1)} %fusion.256) | copy-start | bytes 2368 | tf_op jit(solution)/shard_map/while
  697.0 42.9 %copy-start.19 = (f32[384]{0:T(512)}, f32[384]{0:T(512)S(1)}, u32[]{:S(2)}) copy-start(f32[384]{0:T(512)S(1)} %convert_element_type.530) | copy-start | bytes 4612 | tf_op jit(solution)/shard_map/while
  697.0 47.7 %copy-start.33 = (f32[384]{0:T(512)}, f32[384]{0:T(512)S(1)}, u32[]{:S(2)}) copy-start(f32[384]{0:T(512)S(1)} %convert_element_type.532) | copy-start | bytes 4612 | tf_op jit(solution)/shard_map/while
  697.0 42.9 %copy-start.31 = (f32[384]{0:T(512)}, f32[384]{0:T(512)S(1)}, u32[]{:S(2)}) copy-start(f32[384]{0:T(512)S(1)} %convert_element_type.531) | copy-start | bytes 4612 | tf_op jit(solution)/shard_map/while
  697.8 42.2 %copy-start.26 = (s32[197,1]{0,1:T(1,128)}, s32[197,1]{0,1:T(1,128)S(1)}, u32[]{:S(2)}) copy-start(s32[197,1]{0,1:T(1,128)S(1)} %get-tuple-element.1147) | copy-start | bytes 2368 | tf_op jit(solution)/shard_map/while
  699.2 45.7 %copy-start.63 = (pred[197]{0:T(512)(128)(4,1)}, pred[197]{0:T(512)(128)(4,1)S(1)}, u32[]{:S(2)}) copy-start(pred[197]{0:T(512)(128)(4,1)S(1)} %get-tuple-element.1155) | copy-start | bytes 595 | tf_op jit(solution)/shard_map/while
  699.2 45.7 %copy-start.65 = (pred[197]{0:T(512)(128)(4,1)}, pred[197]{0:T(512)(128)(4,1)S(1)}, u32[]{:S(2)}) copy-start(pred[197]{0:T(512)(128)(4,1)S(1)} %get-tuple-element.1154) | copy-start | bytes 595 | tf_op jit(solution)/shard_map/while
  699.8 91.5 %copy-start.49 = (s32[197,1]{0,1:T(1,128)}, s32[197,1]{0,1:T(1,128)S(1)}, u32[]{:S(2)}) copy-start(s32[197,1]{0,1:T(1,128)S(1)} %get-tuple-element.1153) | copy-start | bytes 2368 | tf_op jit(solution)/shard_map/while
  699.8 92.0 %copy-start.47 = (s32[197,1]{0,1:T(1,128)}, s32[197,1]{0,1:T(1,128)S(1)}, u32[]{:S(2)}) copy-start(s32[197,1]{0,1:T(1,128)S(1)} %get-tuple-element.1152) | copy-start | bytes 2368 | tf_op jit(solution)/shard_map/while
  744.9 45.6 %copy-start.15 = (bf16[197,384]{1,0:T(8,128)(2,1)}, bf16[197,384]{1,0:T(8,128)(2,1)S(1)}, u32[]{:S(2)}) copy-start(bf16[197,384]{1,0:T(8,128)(2,1)S(1)} %add_convert_fusion.9) | copy-start | bytes 453892 | tf_op jit(solution)/shard_map/while
  746.1 27.8 %all-to-all-start = ((bf16[16,2,16,384]{3,2,1,0:T(8,128)(2,1)}), bf16[16,2,16,384]{3,2,1,0:T(8,128)(2,1)S(1)}, u32[]{:S(2)}, u32[]{:S(2)}) async-start(bf16[16,2,16,384]{3,2,1,0:T(8,128)(2,1)} %bitcast.391), calls=%async_computation | async-start | bytes 786432 | tf_op jit(solution)/shard_map/while/body/eval_jaxpr/all_to_all | solution.py:164
  786.2 16.4 %all-to-all-start.1 = ((bf16[16,2,16,384]{3,2,1,0:T(8,128)(2,1)}), bf16[16,2,16,384]{3,2,1,0:T(8,128)(2,1)}, u32[]{:S(2)}, u32[]{:S(2)}) async-start(bf16[16,2,16,384]{3,2,1,0:T(8,128)(2,1)} %copy.159), calls=%async_computation.1 | async-start | bytes 786432 | tf_op jit(solution)/shard_map/while/body/eval_jaxpr/all_to_all | solution.py:167
  816.9 15.7 %all-to-all-start.2 = ((bf16[16,2,16,384]{3,2,1,0:T(8,128)(2,1)}), bf16[16,2,16,384]{3,2,1,0:T(8,128)(2,1)S(1)}, u32[]{:S(2)}, u32[]{:S(2)}) async-start(bf16[16,2,16,384]{3,2,1,0:T(8,128)(2,1)} %bitcast.414), calls=%async_computation.2 | async-start | bytes 786432 | tf_op jit(solution)/shard_map/while/body/eval_jaxpr/all_to_all | solution.py:198
  839.9 16.4 %all-to-all-start.3 = ((bf16[16,2,16,384]{3,2,1,0:T(8,128)(2,1)}), bf16[16,2,16,384]{3,2,1,0:T(8,128)(2,1)}, u32[]{:S(2)}, u32[]{:S(2)}) async-start(bf16[16,2,16,384]{3,2,1,0:T(8,128)(2,1)} %copy.160), calls=%async_computation.3 | async-start | bytes 786432 | tf_op jit(solution)/shard_map/while/body/eval_jaxpr/all_to_all | solution.py:214
  871.5 111.1 %reduce-scatter.12.cloned.1.call-start = ((), (), s32[]{:S(2)}) async-start(), calls=%async_computation.8 | async-start | bytes 313344
  873.4 167.9 %reduce-scatter.10.cloned.1.call-start = ((), (), s32[]{:S(2)}) async-start(), calls=%async_computation.7 | async-start | bytes 940032
  876.0 228.8 %all-reduce.24.cloned.1.call-start = ((), (), s32[]{:S(2)}) async-start(), calls=%async_computation.10 | async-start | bytes 18874368 | tf_op jit(solution)/shard_map/psum | solution.py:301
  (229 other events, 1459.3 us)
Sparse Core Ops, SparseCore 0:
  871.6 54.0 reduce-scatter.13
  929.6 52.8 reduce-scatter.11
  986.2 55.0 reduce-scatter.9
Sparse Core Ops, SparseCore 1:
  879.5 225.2 all-reduce.23
where the time goes:
time: 1120 us
  blocking collectives  434 us (39%)
  waiting for transfers between devices  247 us (22%)
  matrix products  176 us (16%)
  other arithmetic  111 us (10%)
  local copies, waits for them, and re-layouts  65.9 us (6%)
  starting transfers between devices  62.2 us (6%)
  between operations  16.1 us (1%)
    while x4, blocking collectives  133 us
    unnamed x7, waiting for transfers between devices  128 us
    all_gather x4, blocking collectives, micro_step(): lax.all_gather(router_weight, 'fsdp', axis=0, tiled=True)  92.2 us
    all_gather x4, blocking collectives, micro_step(): lax.all_gather(attend_weight, 'fsdp', axis=0, tiled=True)  87.4 us
    all_gather x4, blocking collectives, micro_step(): lax.all_gather(output_weight, 'fsdp', axis=0, tiled=True)  72.9 us
    psum x1, waiting for transfers between devices, body(): lax.psum((shards[0], shards[1], shards[2], shards[3], shards[4], shards[5...  48.4 us
    all_to_all x4, waiting for transfers between devices, micro_step(): lax.all_to_all(produced, 'fsdp', split_axis=0, concat_axis=0, tiled=True)  41.3 us
    dot_general x4, matrix products, expert_work(): jnp.einsum('sxcd,xdf->sxcf', received, expert_up, preferred_element_type=...  41.2 us
  transfers between devices with their start and end apart: 20, of which 16 were waited for; matrix products, arithmetic and copies ran while one was open for 8% of the time, Pallas kernels for 0%

commit v1 on v0

v1 whole, which is shorter than its diff:
```python
import jax
import jax.numpy as jnp
from jax import lax
from jax.sharding import PartitionSpec as P

HEADS = 6
HEAD_DIM = 64
CAP = 16
EPSILON = 1e-06
BF = jnp.bfloat16
F32 = jnp.float32


def dot(a, b, ca, cb):
    return lax.dot_general(a, b, (((ca,), (cb,)), ((), ())), preferred_element_type=F32)


def layer_norm(values, gain, shift):
    center = values - jnp.mean(values, axis=-1, keepdims=True)
    spread = jnp.mean(center * center, axis=-1, keepdims=True)
    return center * lax.rsqrt(spread + EPSILON) * gain + shift


def norm_parts(values):
    center = values - jnp.mean(values, axis=-1, keepdims=True)
    inv = lax.rsqrt(jnp.mean(center * center, axis=-1, keepdims=True) + EPSILON)
    return center * inv, inv


def norm_back(grad, hat, inv, gain):
    scaled = grad * gain
    return inv * (
        scaled
        - jnp.mean(scaled, axis=-1, keepdims=True)
        - hat * jnp.mean(scaled * hat, axis=-1, keepdims=True)
    )


def route(picks, ranks, capacity):
    labels = jnp.arange(capacity.shape[0], dtype=jnp.int32)
    earlier = (ranks[None, :] < ranks[:, None]).astype(BF)
    hits = [(picks[:, c, None] == labels[None, :]) for c in range(2)]
    ones = [h.astype(BF) for h in hits]
    before = [dot(earlier, ones[0], 1, 0)]
    before.append(dot(earlier, ones[1], 1, 0) + jnp.sum(ones[0].astype(F32), 0, keepdims=True))
    slots = []
    for c in range(2):
        position = jnp.sum(jnp.where(hits[c], before[c], 0.0), axis=1).astype(jnp.int32)
        limit = jnp.sum(jnp.where(hits[c], capacity[None, :], 0), axis=1)
        slots.append(jnp.where(position < limit, picks[:, c] * CAP + position, -1))
    return slots


def solution(mesh):
    replicas = mesh.shape["replica"]

    def body(tokens_in, picks_in, ranks_in, capacity, first_gain, first_shift, attend_weight,
             output_weight, second_gain, second_shift, router_weight, expert_up, expert_down, cotangent):
        micro, _, length, width = tokens_in.shape
        experts = capacity.shape[0]
        groups = lax.axis_size("fsdp")
        local = expert_up.shape[0]
        slots = experts * CAP
        scale = HEAD_DIM ** (-0.5)
        packed = jnp.concatenate(
            [attend_weight, output_weight, router_weight]
            + [v[:, None] for v in (first_gain, first_shift, second_gain, second_shift)], axis=1)
        cols = packed.shape[1]
        packed = jnp.pad(packed, ((0, 0), (0, -cols % 128)))
        full = lax.all_gather(packed, "fsdp", axis=0, tiled=True)
        attend = full[:, : 3 * width]
        output = full[:, 3 * width : 4 * width]
        router = full[:, 4 * width : 4 * width + experts]
        vecs = full[:, 4 * width + experts : cols].astype(F32).T
        gain_one, shift_one, gain_two, shift_two = (vecs[i][None] for i in range(4))

        tokens = tokens_in[:, 0].astype(F32)
        incoming = cotangent[:, 0].astype(F32)
        slot_ids = jax.vmap(lambda p, r: route(p, r, capacity))(picks_in[:, 0], ranks_in[:, 0])
        rows = jnp.arange(slots, dtype=jnp.int32)
        table = ((slot_ids[0][:, None, :] == rows[None, :, None])
                 | (slot_ids[1][:, None, :] == rows[None, :, None])).astype(BF)

        def exchange(rows_):
            r = rows_.reshape(micro, groups, local * CAP, width).transpose(1, 0, 2, 3)
            return lax.all_to_all(r, "fsdp", split_axis=0, concat_axis=0, tiled=True)

        def come_back(r):
            r = lax.all_to_all(r, "fsdp", split_axis=0, concat_axis=0, tiled=True)
            return r.transpose(1, 0, 2, 3).reshape(micro, slots, width)

        def pick_rows(v):
            return jnp.einsum("mst,mtd->msd", table, v, preferred_element_type=F32).astype(BF)

        def to_expert(r):
            return r.reshape(groups, micro, local, CAP, width).transpose(2, 0, 1, 3, 4).reshape(local, -1, width)

        def from_expert(r):
            return r.reshape(local, groups, micro, CAP, width).transpose(1, 2, 0, 3, 4).reshape(
                groups, micro, local * CAP, width)

        def swap(v):
            return lax.ppermute(v, "replica", [(0, 1), (1, 0)])

        cot_rows = exchange(pick_rows(cotangent[:, 0]))

        hat_one, inv_one = norm_parts(tokens)
        normed = (hat_one * gain_one + shift_one).astype(BF)
        joined = jnp.einsum("mtd,de->mte", normed, attend, preferred_element_type=F32).astype(BF)
        heads = joined.reshape(micro, length, 3, HEADS, HEAD_DIM)
        queries, keys, values = heads[:, :, 0], heads[:, :, 1], heads[:, :, 2]
        scores = jnp.einsum("mqhd,mkhd->mhqk", queries, keys, preferred_element_type=F32) * scale
        raised = jnp.exp(scores - jnp.max(scores, axis=-1, keepdims=True))
        probs = raised / jnp.sum(raised, axis=-1, keepdims=True)
        probs_low = probs.astype(BF)
        mixed = jnp.einsum("mhqk,mkhd->mqhd", probs_low, values, preferred_element_type=F32)
        mixed = mixed.reshape(micro, length, width).astype(BF)
        middle = tokens + jnp.einsum("mtd,de->mte", mixed, output, preferred_element_type=F32)
        hat_two, inv_two = norm_parts(middle)
        second = (hat_two * gain_two + shift_two).astype(BF)
        rows_in = exchange(pick_rows(second))

        x = to_expert(rows_in)
        gx = to_expert(cot_rows)
        first_label = lax.axis_index("fsdp") * local
        own = jnp.arange(experts)[None, :] == (first_label + jnp.arange(local))[:, None]

        def up_side(x, gx):
            logits = jnp.einsum("xrd,de->xre", x, router, preferred_element_type=F32)
            gates = jax.nn.softmax(logits, axis=-1)
            gate = jnp.sum(jnp.where(own[:, None, :], gates, 0.0), axis=-1, keepdims=True)
            back = (gate * gx.astype(F32)).astype(BF)
            pre = jnp.einsum("xrd,xdf->xrf", x, expert_up, preferred_element_type=F32)
            hidden, pull = jax.vjp(lambda v: jax.nn.gelu(v, approximate=False), pre)
            hidden = hidden.astype(BF)
            hidden_grad = jnp.einsum("xrd,xfd->xrf", back, expert_down, preferred_element_type=F32)
            pre_grad = pull(hidden_grad)[0].astype(BF)
            return gates, gate, back, hidden, pre_grad

        gates, gate, back, hidden, pre_grad = up_side(x, gx)
        produced = jnp.einsum("xrf,xfd->xrd", hidden, expert_down, preferred_element_type=F32)
        weighted = (gate * produced).astype(BF)
        gate_grad = jnp.sum(gx.astype(F32) * produced, axis=-1, keepdims=True)
        logits_grad = (gates * (jnp.where(own[:, None, :], gate_grad, 0.0) - gate * gate_grad)).astype(BF)
        row_grad = (jnp.einsum("xrf,xdf->xrd", pre_grad, expert_up, preferred_element_type=F32)
                    + jnp.einsum("xre,de->xrd", logits_grad, router, preferred_element_type=F32)).astype(BF)
        router_grad = jnp.einsum("xrd,xre->de", x, logits_grad, preferred_element_type=F32)
        if replicas == 2:
            x2, gx2 = to_expert(swap(rows_in)), to_expert(swap(cot_rows))
            _, _, back2, hidden2, pre_grad2 = up_side(x2, gx2)
            cat = lambda a, b: jnp.concatenate([a, b], axis=1)
        else:
            x2, back2, hidden2, pre_grad2 = x, back, hidden, pre_grad
            cat = lambda a, b: a
        down_grad = jnp.einsum("xrf,xrd->xfd", cat(hidden, hidden2), cat(back, back2), preferred_element_type=F32)
        up_grad = jnp.einsum("xrd,xrf->xdf", cat(x, x2), cat(pre_grad, pre_grad2), preferred_element_type=F32)
        if replicas != 2:
            up_grad, down_grad = lax.psum((up_grad, down_grad), "replica")

        second_rows = come_back(from_expert(row_grad))
        result_rows = come_back(from_expert(weighted))
        second_grad = jnp.einsum("mst,msd->mtd", table, second_rows, preferred_element_type=F32)
        out = (middle + jnp.einsum("mst,msd->mtd", table, result_rows, preferred_element_type=F32)).astype(BF)

        gain_two_grad = jnp.sum(second_grad * hat_two, axis=(0, 1))
        shift_two_grad = jnp.sum(second_grad, axis=(0, 1))
        middle_grad = incoming + norm_back(second_grad, hat_two, inv_two, gain_two)
        branch_grad = middle_grad.astype(BF)
        output_grad = jnp.einsum("mtd,mte->de", mixed, branch_grad, preferred_element_type=F32)
        mixed_grad = jnp.einsum("mte,de->mtd", branch_grad, output, preferred_element_type=F32).astype(BF)
        mixed_grad = mixed_grad.reshape(micro, length, HEADS, HEAD_DIM)
        values_grad = jnp.einsum("mhqk,mqhd->mkhd", probs_low, mixed_grad, preferred_element_type=F32).astype(BF)
        probs_grad = jnp.einsum("mqhd,mkhd->mhqk", mixed_grad, values, preferred_element_type=F32)
        scores_grad = (probs * (probs_grad - jnp.sum(probs * probs_grad, axis=-1, keepdims=True))).astype(BF)
        queries_grad = (jnp.einsum("mhqk,mkhd->mqhd", scores_grad, keys, preferred_element_type=F32) * scale).astype(BF)
        keys_grad = (jnp.einsum("mhqk,mqhd->mkhd", scores_grad, queries, preferred_element_type=F32) * scale).astype(BF)
        joined_grad = jnp.stack([queries_grad, keys_grad, values_grad], axis=2).reshape(micro, length, 3 * width)
        attend_grad = jnp.einsum("mtd,mte->de", normed, joined_grad, preferred_element_type=F32)
        normed_grad = jnp.einsum("mte,de->mtd", joined_grad, attend, preferred_element_type=F32)
        gain_one_grad = jnp.sum(normed_grad * hat_one, axis=(0, 1))
        shift_one_grad = jnp.sum(normed_grad, axis=(0, 1))
        tokens_grad = (middle_grad + norm_back(normed_grad, hat_one, inv_one, gain_one)).astype(BF)

        grads = jnp.concatenate(
            [attend_grad, output_grad, router_grad,
             jnp.stack([gain_one_grad, shift_one_grad, gain_two_grad, shift_two_grad], axis=1)], axis=1).astype(BF)
        grads = jnp.pad(grads, ((0, 0), (0, -cols % 128))).reshape(groups, width // groups, -1)
        grads = lax.all_to_all(grads, "fsdp", split_axis=0, concat_axis=0, tiled=True)
        share = jnp.sum(grads.astype(F32), axis=0)
        share = lax.psum(share, "replica")
        w = 4 * width
        return (out[:, None], tokens_grad[:, None], share[:, w + experts], share[:, w + experts + 1],
                share[:, : 3 * width], share[:, 3 * width : w], share[:, w + experts + 2],
                share[:, w + experts + 3], share[:, w : w + experts], up_grad, down_grad)

    split = ("replica", "fsdp")
    in_specs = (P(None, split), P(None, split), P(None, split), P(), P("fsdp"), P("fsdp"), P("fsdp"), P("fsdp"),
                P("fsdp"), P("fsdp"), P("fsdp"), P("fsdp"), P("fsdp"), P(None, split))
    out_specs = (P(None, split), P(None, split)) + (P("fsdp"),) * 9
    return jax.shard_map(body, mesh=mesh, in_specs=in_specs, out_specs=out_specs, check_vma=False)
```

time: 1120 us -> 413 us (0.37)
  blocking collectives: 434 us -> 0 us
  waiting for transfers between devices: 247 us -> 110 us
  other arithmetic: 111 us -> 51.2 us
  matrix products: 176 us -> 144 us
  starting transfers between devices: 62.2 us -> 37.2 us
  local copies, waits for them, and re-layouts: 65.9 us -> 46.7 us
    all_gather x12 -> x0, blocking collectives: 252 us -> none  [the longest x4 92.2 us: micro_step(): lax.all_gather(router_weight, 'fsdp', axis=0, tiled=True)]
    while x4 -> x0, blocking collectives: 133 us -> none
    unnamed x7 -> x2, waiting for transfers between devices: 128 us -> 0.03 us
    all_to_all x16 -> x5, waiting for transfers between devices: 70.9 us -> 16 us  [the longest x1 11 us: body(): lax.all_to_all(grads, 'fsdp', split_axis=0, concat_axis=0, tiled=True)]
    all_gather x0 -> x1, waiting for transfers between devices: none -> 41.5 us  [body(): full = lax.all_gather(packed, 'fsdp', axis=0, tiled=True)]
    dot_general x92 -> x29, matrix products: 176 us -> 142 us  [the longest x2 43.4 us: up_side(): pre = jnp.einsum('xrd,xdf->xrf', x, expert_up, preferred_element_type=F32)]
    unnamed x1 -> x0, blocking collectives: 33.4 us -> none
    ppermute x0 -> x2, waiting for transfers between devices: none -> 31.5 us  [swap(): return lax.ppermute(v, 'replica', [(0, 1), (1, 0)])]
  transfers between devices with their start and end apart: 20 -> 9, of which waited for: 16 -> 5; matrix products, arithmetic and copies ran while one was open for 8% -> 44% of each run, Pallas kernels for 0% -> 0%
where the time goes in v1:
time: 413 us; the launch traced here: 405 us
  matrix products  144 us (35%)
  waiting for transfers between devices  110 us (27%)
  other arithmetic  51.2 us (12%)
  local copies, waits for them, and re-layouts  46.7 us (11%)
  starting transfers between devices  37.2 us (9%)
  between operations  15.2 us (4%)
    dot_general x2, matrix products, up_side(): pre = jnp.einsum('xrd,xdf->xrf', x, expert_up, preferred_element_type=F32)  43.4 us
    all_gather x1, waiting for transfers between devices, body(): full = lax.all_gather(packed, 'fsdp', axis=0, tiled=True)  41.5 us
    ppermute x2, waiting for transfers between devices, swap(): return lax.ppermute(v, 'replica', [(0, 1), (1, 0)])  31.5 us
    convert_element_type x1, other arithmetic, up_side(): hidden = hidden.astype(BF)  31 us
    dot_general x2, matrix products, up_side(): jnp.einsum('xrd,xfd->xrf', back, expert_down, preferred_element_type=F32)  26.7 us
    psum x1, waiting for transfers between devices, body(): share = lax.psum(share, 'replica')  21 us
    all_to_all x2, starting transfers between devices, come_back(): r = lax.all_to_all(r, 'fsdp', split_axis=0, concat_axis=0, tiled=True)  12.8 us
    dot_general x1, matrix products, body(): jnp.einsum('xrf,xrd->xfd', cat(hidden, hidden2), cat(back, back2), prefer...  12.4 us
  transfers between devices with their start and end apart: 9, of which 5 were waited for; matrix products, arithmetic and copies ran while one was open for 44% of the time, Pallas kernels for 0%

profile of v1, /device:TPU:0, one launch (start us, length us, event | category | flops | bytes accessed | tf_op | source)
XLA Modules:
  0.0 404.8 jit_solution(912585068217284608)
XLA Ops:
  15.1 2.3 convolution_convert_fusion.1
  17.4 1.4 copy.237
  18.8 7.4 %all-to-all-start.2 = ((bf16[16,4,32,384]{3,2,1,0:T(8,128)(2,1)}), bf16[16,4,32,384]{3,2,1,0:T(8,128)(2,1)}, u32[]{:S(2)}, u32[]{:S(2)}) async-start(bf16[16,4,32,384]{3,2,1,0:T(8,128)(2,1)} %bitcast.224), calls=%async_computation.2 | async-start | bytes 3145728 | tf_op jit(solution)/shard_map/all_to_all | solution.py:86
  26.9 41.5 %all-gather.2.cloned.1.call-done = bf16[384,1664]{1,0:T(8,128)(2,1)} async-done(((bf16[24,1664]{1,0:T(8,128)(2,1)}), bf16[384,1664]{1,0:T(8,128)(2,1)}) %all-gather.2.cloned.1.call-update) | async-done | bytes 1277968 | tf_op jit(solution)/shard_map/all_gather | solution.py:70
  68.5 1.0 convert_bitcast_fusion.3
  70.5 3.7 convolution_convert_fusion
  74.2 4.1 %copy.146 = bf16[4,197,1152]{1,2,0:T(8,128)(2,1)} copy(bf16[4,197,1152]{2,1,0:T(8,128)(2,1)} %convolution_convert_fusion) | data formatting | bytes 3631104 | tf_op jit(solution)/shard_map/convert_element_type | solution.py:109
  78.3 2.2 fusion.85
  80.5 4.1 %fusion.133 = (f32[4,6,197]{2,1,0:T(8,128)S(1)}, f32[4,6,197,197]{2,3,1,0:T(8,128)S(1)}) fusion(f32[4,6,197,197]{2,3,1,0:T(8,128)S(1)} %fusion.85), kind=kOutput, calls=%fused_computation.230 | output fusion | flops 3725860 | bytes 7470240 | tf_op jit(solution)/shard_map/sub | solution.py:113
  84.7 2.4 convolution_convert_fusion.4
  87.0 1.9 fusion.134
  90.0 1.6 convolution_convert_fusion.2
  91.7 1.4 copy.238
  93.1 4.6 %all-to-all-start = ((bf16[16,4,32,384]{3,2,1,0:T(8,128)(2,1)}), bf16[16,4,32,384]{3,2,1,0:T(8,128)(2,1)}, u32[]{:S(2)}, u32[]{:S(2)}) async-start(bf16[16,4,32,384]{3,2,1,0:T(8,128)(2,1)} %bitcast.225), calls=%async_computation | async-start | bytes 3145728 | tf_op jit(solution)/shard_map/all_to_all | solution.py:86
  97.8 1.6 collective-permute-start.1
  99.4 1.8 convert_bitcast_fusion.1
  101.2 2.1 copy.160
  103.3 31.5 %collective-permute-done.1 = bf16[16,4,32,384]{3,2,1,0:T(8,128)(2,1)} collective-permute-done((bf16[16,4,32,384]{3,2,1,0:T(8,128)(2,1)}, bf16[16,4,32,384]{3,2,1,0:T(8,128)(2,1)}, u32[]{:S(2)}, u32[]{:S(2)}) %collective-permute-start.1) | collective-permute-done | bytes 1572896 | tf_op jit(solution)/shard_map/ppermute | solution.py:103
  134.8 1.8 convert_bitcast_fusion
  136.7 2.1 copy.180
  138.8 1.7 copy.154
  140.5 1.6 fusion.125
  142.7 10.5 %fusion.38 = (u8[1024,1536]{1,0:T(8,128)(4,1)S(1)}, u8[1024,1536]{1,0:T(8,128)(4,1)S(1)}, f32[2,1024,1536]{2,1,0:T(8,128)}) fusion(bf16[2,1024,384]{2,1,0:T(8,128)(2,1)S(1)} %bitcast.229, bf16[2,384,1536]{2,1,0:T(8,128)(2,1)S(1)} %copy-done), kind=kOutput, calls=%fused_computation.74 | convolution fusion | flops 2453667840 | bytes 19660800 | tf_op jit(solution)/shard_map/xrd,xdf->xrf/dot_general | solution.py:133
  153.4 31.0 %multiply_convert_fusion.1 = (bf16[2,1024,1536]{2,1,0:T(8,128)(2,1)S(1)}, f32[2,1024,1536]{2,1,0:T(8,128)}) fusion(f32[2,1024,1536]{2,1,0:T(8,128)} %get-tuple-element.88, u8[1024,1536]{1,0:T(8,128)(4,1)S(1)} %get-tuple-element.56, u8[1024,1536]{1,0:T(8,128)(4,1)S(1)} %get-tuple-element.55), kind=kLoop, calls=%fused_computation.37 | loop fusion | flops 220200960 | bytes 34603008 | tf_op jit(solution)/shard_map/convert_element_type | solution.py:135
  184.4 3.5 fusion.36
  188.0 1.5 collective-permute-start
  189.5 13.3 %add_convert_fusion.1 = bf16[2,1024,1536]{2,1,0:T(8,128)(2,1)} fusion(f32[2,1024,1536]{2,1,0:T(8,128)} %get-tuple-element.78, f32[2,1024,1536]{2,1,0:T(8,128)} %get-tuple-element.88, bf16[2,1024,384]{2,1,0:T(8,128)(2,1)S(1)} %get-tuple-element.80, bf16[2,1536,384]{2,1,0:T(8,128)(2,1)S(1)} %copy-done.44), kind=kOutput, calls=%fused_computation.36 | convolution fusion | flops 2459959296 | bytes 35389440 | tf_op jit(solution)/shard_map/xrd,xfd->xrf/dot_general | solution.py:136
  202.8 1.3 copy.156
  204.2 1.8 fusion.80
  206.7 7.9 %fusion.138 = f32[2,1024,384]{2,1,0:T(8,128)} fusion(bf16[2,1024,1536]{2,1,0:T(8,128)(2,1)} %add_convert_fusion.1, bf16[2,384,1536]{2,1,0:T(8,128)(2,1)S(1)} %copy-done), kind=kOutput, calls=%fused_computation.235 | convolution fusion | flops 2415919104 | bytes 11796480 | tf_op jit(solution)/shard_map/xrf,xdf->xrd/dot_general | solution.py:145
  214.6 3.8 add_convert_fusion.2
  218.4 2.7 copy.162
  221.1 6.4 %all-to-all-start.3 = ((bf16[16,4,32,384]{3,2,1,0:T(8,128)(2,1)}), bf16[16,4,32,384]{3,2,1,0:T(8,128)(2,1)}, u32[]{:S(2)}, u32[]{:S(2)}) async-start(bf16[16,4,32,384]{3,2,1,0:T(8,128)(2,1)} %bitcast.226), calls=%async_computation.3 | async-start | bytes 3145728 | tf_op jit(solution)/shard_map/all_to_all | solution.py:89
  227.5 1.7 copy.178
  229.2 1.2 copy-done.15
  230.3 32.9 %multiply_convert_fusion = (bf16[2,1024,1536]{2,1,0:T(8,128)(2,1)}, f32[2,1024,1536]{2,1,0:T(8,128)}, f32[2,1024,1536]{2,1,0:T(8,128)}) fusion(bf16[2,1024,384]{2,1,0:T(8,128)(2,1)S(1)} %bitcast.234, bf16[2,384,1536]{2,1,0:T(8,128)(2,1)S(1)} %copy-done), kind=kOutput, calls=%fused_computation.22 | convolution fusion | flops 2620391424 | bytes 35389440 | tf_op jit(solution)/shard_map/xrd,xdf->xrf/dot_general | solution.py:133
  263.2 2.1 fusion.137
  265.3 2.4 fusion.34
  267.9 13.4 %add_convert_fusion = bf16[2,1024,1536]{2,1,0:T(8,128)(2,1)} fusion(f32[2,1024,1536]{2,1,0:T(8,128)} %get-tuple-element.76, f32[2,1024,1536]{2,1,0:T(8,128)} %get-tuple-element.95, bf16[2,1024,384]{2,1,0:T(8,128)(2,1)S(1)} %fusion.34, bf16[2,1536,384]{2,1,0:T(8,128)(2,1)S(1)} %copy-done.45), kind=kOutput, calls=%fused_computation.23 | convolution fusion | flops 2459959296 | bytes 35389440 | tf_op jit(solution)/shard_map/xrd,xfd->xrf/dot_general | solution.py:136
  281.3 9.6 %fusion.7 = f32[2,384,1536]{2,1,0:T(8,128)} fusion(bf16[2,1024,1536]{2,1,0:T(8,128)(2,1)} %add_convert_fusion, bf16[2,1024,1536]{2,1,0:T(8,128)(2,1)} %add_convert_fusion.1, bf16[2,1024,384]{2,1,0:T(8,128)(2,1)S(1)} %bitcast.236, bf16[2,1024,384]{2,1,0:T(8,128)(2,1)S(1)} %bitcast.231), kind=kOutput, calls=%fused_computation.14 | convolution fusion | flops 4863295488 | bytes 20447232 | tf_op jit(solution)/shard_map/xrd,xrf->xdf/dot_general | solution.py:156
  290.9 6.5 %all-to-all-start.1 = ((bf16[16,4,32,384]{3,2,1,0:T(8,128)(2,1)}), bf16[16,4,32,384]{3,2,1,0:T(8,128)(2,1)}, u32[]{:S(2)}, u32[]{:S(2)}) async-start(bf16[16,4,32,384]{3,2,1,0:T(8,128)(2,1)} %bitcast.25), calls=%async_computation.1 | async-start | bytes 3145728 | tf_op jit(solution)/shard_map/all_to_all | solution.py:89
  297.4 1.7 copy.163
  299.2 1.9 multiply_reduce_fusion.2
  302.0 1.9 convolution_convert_fusion.5
  303.9 1.2 copy.164
  305.0 4.0 multiply_reduce_fusion
  314.7 2.9 fusion.62
  318.5 2.5 fusion.39
  321.0 2.2 concatenate.20
  323.2 1.2 pad.9
  324.4 5.1 %all-to-all-done.1 = bf16[16,4,32,384]{3,2,1,0:T(8,128)(2,1)} async-done(((bf16[16,4,32,384]{3,2,1,0:T(8,128)(2,1)}), bf16[16,4,32,384]{3,2,1,0:T(8,128)(2,1)}, u32[]{:S(2)}, u32[]{:S(2)}) %all-to-all-start.1) | async-done | bytes 1572896 | tf_op jit(solution)/shard_map/all_to_all | solution.py:89
  329.4 9.1 %all-to-all-start.4 = ((bf16[16,24,1664]{2,1,0:T(8,128)(2,1)}), bf16[16,24,1664]{2,1,0:T(8,128)(2,1)}, u32[]{:S(2)}, u32[]{:S(2)}) async-start(bf16[16,24,1664]{2,1,0:T(8,128)(2,1)} %bitcast.55), calls=%async_computation.4 | async-start | bytes 2555904 | tf_op jit(solution)/shard_map/all_to_all | solution.py:188
  338.6 12.4 %fusion.11 = f32[2,1536,384]{2,1,0:T(8,128)} fusion(bf16[2,1024,1536]{2,1,0:T(8,128)(2,1)} %get-tuple-element.75, bf16[2,1024,1536]{2,1,0:T(8,128)(2,1)} %copy-done.7, bf16[2,1024,384]{2,1,0:T(8,128)(2,1)} %copy-done.17, bf16[2,1024,384]{2,1,0:T(8,128)(2,1)} %copy-done.46), kind=kOutput, calls=%fused_computation.18 | convolution fusion | flops 4863295488 | bytes 20447232 | tf_op jit(solution)/shard_map/xrf,xrd->xfd/dot_general | solution.py:155
  351.1 1.6 copy.157
  353.5 1.1 copy.183
  354.5 11.0 %all-to-all-done.4 = bf16[16,24,1664]{2,1,0:T(8,128)(2,1)} async-done(((bf16[16,24,1664]{2,1,0:T(8,128)(2,1)}), bf16[16,24,1664]{2,1,0:T(8,128)(2,1)}, u32[]{:S(2)}, u32[]{:S(2)}) %all-to-all-start.4) | async-done | bytes 1277984 | tf_op jit(solution)/shard_map/all_to_all | solution.py:188
  365.5 2.1 convert_reduce_fusion
  367.7 2.2 fusion.89
  369.8 1.1 copy.184
  370.9 21.0 %all-reduce.4.cloned.1.call-done = f32[24,1664]{1,0:T(8,128)} async-done(((f32[24,1664]{1,0:T(8,128)}), f32[24,1664]{1,0:T(8,128)}) %all-reduce.4.cloned.1.call-update) | async-done | bytes 159760 | tf_op jit(solution)/shard_map/psum | solution.py:190
  391.9 1.6 slice_reduce_fusion.4
  393.5 1.3 slice.101
  394.8 1.4 slice.98
  396.2 1.5 slice.97
  (152 shorter events, 20.5 us)
Async XLA Ops:
  7.2 135.6 %copy-start = (bf16[2,384,1536]{2,1,0:T(8,128)(2,1)S(1)}, bf16[2,384,1536]{2,1,0:T(8,128)(2,1)}, u32[]{:S(2)}) copy-start(bf16[2,384,1536]{2,1,0:T(8,128)(2,1)} %param.25) | copy-start | bytes 7077892
  7.2 61.3 %all-gather.2.cloned.1.call-start = ((), (), s32[]{:S(2)}) async-start(), calls=%async_computation.5 | async-start | bytes 1357824 | tf_op jit(solution)/shard_map/all_gather | solution.py:70
  15.1 74.3 %copy-start.38 = (s32[4,197]{1,0:T(4,128)}, s32[4,197]{1,0:T(4,128)S(1)}, u32[]{:S(2)}) copy-start(s32[4,197]{1,0:T(4,128)S(1)} %add_select_fusion.1) | copy-start | bytes 9460
  15.1 74.3 %copy-start.40 = (s32[4,197]{1,0:T(4,128)}, s32[4,197]{1,0:T(4,128)S(1)}, u32[]{:S(2)}) copy-start(s32[4,197]{1,0:T(4,128)S(1)} %add_select_fusion) | copy-start | bytes 9460
  15.1 11.1 %copy-start.8 = (bf16[4,1,197,384]{3,0,2,1:T(4,128)(2,1)S(1)}, bf16[4,1,197,384]{3,0,2,1:T(4,128)(2,1)}, u32[]{:S(2)}) copy-start(bf16[4,1,197,384]{3,0,2,1:T(4,128)(2,1)} %param.14) | copy-start | bytes 1815556
  18.8 74.4 %all-to-all-start.2 = ((bf16[16,4,32,384]{3,2,1,0:T(8,128)(2,1)}), bf16[16,4,32,384]{3,2,1,0:T(8,128)(2,1)}, u32[]{:S(2)}, u32[]{:S(2)}) async-start(bf16[16,4,32,384]{3,2,1,0:T(8,128)(2,1)} %bitcast.224), calls=%async_computation.2 | async-start | bytes 3145728 | tf_op jit(solution)/shard_map/all_to_all | solution.py:86
  26.5 51.8 %copy-start.28 = (f32[4,197]{1,0:T(4,128)}, f32[4,197]{1,0:T(4,128)S(1)}, u32[]{:S(2)}) copy-start(f32[4,197]{1,0:T(4,128)S(1)} %broadcast_multiply_fusion.5) | copy-start | bytes 9460
  26.9 51.3 %copy-start.32 = (f32[4,197]{1,0:T(4,128)}, f32[4,197]{1,0:T(4,128)S(1)}, u32[]{:S(2)}) copy-start(f32[4,197]{1,0:T(4,128)S(1)} %add_rsqrt_fusion.1) | copy-start | bytes 9460
  69.9 0.5 copy-start.34
  69.9 0.6 copy-start.42
  69.9 19.5 %copy-start.36 = (f32[384]{0:T(512)}, f32[384]{0:T(512)S(1)}, u32[]{:S(2)}) copy-start(f32[384]{0:T(512)S(1)} %get-tuple-element.65) | copy-start | bytes 4612
  84.6 2.4 copy-start.3
  84.6 2.4 copy-start.24
  87.0 2.4 copy-start.18
  89.0 1.1 copy-start.10
  89.0 2.7 copy-start.26
  89.4 2.3 copy-start.30
  93.1 45.6 %all-to-all-start = ((bf16[16,4,32,384]{3,2,1,0:T(8,128)(2,1)}), bf16[16,4,32,384]{3,2,1,0:T(8,128)(2,1)}, u32[]{:S(2)}, u32[]{:S(2)}) async-start(bf16[16,4,32,384]{3,2,1,0:T(8,128)(2,1)} %bitcast.225), calls=%async_computation | async-start | bytes 3145728 | tf_op jit(solution)/shard_map/all_to_all | solution.py:86
  97.8 37.1 %collective-permute-start.1 = (bf16[16,4,32,384]{3,2,1,0:T(8,128)(2,1)}, bf16[16,4,32,384]{3,2,1,0:T(8,128)(2,1)}, u32[]{:S(2)}, u32[]{:S(2)}) collective-permute-start(bf16[16,4,32,384]{3,2,1,0:T(8,128)(2,1)} %all-to-all-done.2), channel_id=1, source_target_pairs={{0,16},{16,0},{1,17},{17,1},{2,18},{18,2},{3,19},{19,3},{4,20},{20... | collective-permute-start | bytes 4718600 | tf_op jit(solution)/shard_map/ppermute | solution.py:103
  140.4 12.8 %copy-start.5 = (bf16[16,4,2,16,384]{4,3,1,0,2:T(8,128)(2,1)}, bf16[16,4,2,16,384]{4,3,1,0,2:T(8,128)(2,1)S(1)}, u32[]{:S(2)}) copy-start(bf16[16,4,2,16,384]{4,3,1,0,2:T(8,128)(2,1)S(1)} %copy.154) | copy-start | bytes 4718596
  153.4 31.0 %copy-start.14 = (f32[2,16,4,16,384]{4,3,2,1,0:T(8,128)S(1)}, f32[2,16,4,16,384]{4,3,2,1,0:T(8,128)}, u32[]{:S(2)}) copy-start(f32[2,16,4,16,384]{4,3,2,1,0:T(8,128)} %copy.160) | copy-start | bytes 9437188
  153.4 31.0 %copy-start.44 = (bf16[2,1536,384]{2,1,0:T(8,128)(2,1)S(1)}, bf16[2,1536,384]{2,1,0:T(8,128)(2,1)}, u32[]{:S(2)}) copy-start(bf16[2,1536,384]{2,1,0:T(8,128)(2,1)} %param.26) | copy-start | bytes 7077892
  184.4 3.5 copy-start.7
  188.0 14.9 %copy-start.46 = (bf16[2,1024,384]{2,1,0:T(8,128)(2,1)}, bf16[2,1024,384]{2,1,0:T(8,128)(2,1)S(1)}, u32[]{:S(2)}) copy-start(bf16[2,1024,384]{2,1,0:T(8,128)(2,1)S(1)} %get-tuple-element.80) | copy-start | bytes 4718596
  188.0 39.5 %collective-permute-start = (bf16[16,4,32,384]{3,2,1,0:T(8,128)(2,1)}, bf16[16,4,32,384]{3,2,1,0:T(8,128)(2,1)}, u32[]{:S(2)}, u32[]{:S(2)}) collective-permute-start(bf16[16,4,32,384]{3,2,1,0:T(8,128)(2,1)} %all-to-all-done), channel_id=1, source_target_pairs={{0,16},{16,0},{1,17},{17,1},{2,18},{18,2},{3,19},{19,3},{4,20},{20... | collective-permute-start | bytes 4718600 | tf_op jit(solution)/shard_map/ppermute | solution.py:103
  221.1 69.8 %all-to-all-start.3 = ((bf16[16,4,32,384]{3,2,1,0:T(8,128)(2,1)}), bf16[16,4,32,384]{3,2,1,0:T(8,128)(2,1)}, u32[]{:S(2)}, u32[]{:S(2)}) async-start(bf16[16,4,32,384]{3,2,1,0:T(8,128)(2,1)} %bitcast.226), calls=%async_computation.3 | async-start | bytes 3145728 | tf_op jit(solution)/shard_map/all_to_all | solution.py:89
  229.2 1.2 copy-start.15
  265.2 2.6 copy-start.45
  267.6 13.6 %copy-start.17 = (bf16[2,1024,384]{2,1,0:T(8,128)(2,1)}, bf16[2,1024,384]{2,1,0:T(8,128)(2,1)S(1)}, u32[]{:S(2)}) copy-start(bf16[2,1024,384]{2,1,0:T(8,128)(2,1)S(1)} %fusion.34) | copy-start | bytes 4718596
  267.9 13.4 %copy-start.6 = (bf16[16,4,2,16,384]{4,3,1,0,2:T(8,128)(2,1)S(1)}, bf16[16,4,2,16,384]{4,3,1,0,2:T(8,128)(2,1)}, u32[]{:S(2)}) copy-start(bf16[16,4,2,16,384]{4,3,1,0,2:T(8,128)(2,1)} %copy-done.5) | copy-start | bytes 4718596
  267.9 13.4 %copy-start.16 = (bf16[16,4,2,16,384]{4,3,1,0,2:T(8,128)(2,1)S(1)}, bf16[16,4,2,16,384]{4,3,1,0,2:T(8,128)(2,1)}, u32[]{:S(2)}) copy-start(bf16[16,4,2,16,384]{4,3,1,0,2:T(8,128)(2,1)} %copy-done.15) | copy-start | bytes 4718596
  290.9 8.3 %copy-start.11 = (f32[4,197,384]{2,1,0:T(8,128)S(1)}, f32[4,197,384]{2,1,0:T(8,128)}, u32[]{:S(2)}) copy-start(f32[4,197,384]{2,1,0:T(8,128)} %copy-done.10) | copy-start | bytes 3631108
  290.9 8.3 %copy-start.27 = (f32[4,197]{1,0:T(4,128)S(1)}, f32[4,197]{1,0:T(4,128)}, u32[]{:S(2)}) copy-start(f32[4,197]{1,0:T(4,128)} %copy-done.26) | copy-start | bytes 9460
  290.9 8.3 %copy-start.31 = (f32[4,197]{1,0:T(4,128)S(1)}, f32[4,197]{1,0:T(4,128)}, u32[]{:S(2)}) copy-start(f32[4,197]{1,0:T(4,128)} %copy-done.30) | copy-start | bytes 9460
  290.9 8.3 %copy-start.37 = (f32[384]{0:T(512)S(1)}, f32[384]{0:T(512)}, u32[]{:S(2)}) copy-start(f32[384]{0:T(512)} %copy-done.36) | copy-start | bytes 4612
  290.9 8.3 %copy-start.39 = (s32[4,197]{1,0:T(4,128)S(1)}, s32[4,197]{1,0:T(4,128)}, u32[]{:S(2)}) copy-start(s32[4,197]{1,0:T(4,128)} %copy-done.38) | copy-start | bytes 9460
  290.9 8.3 %copy-start.41 = (s32[4,197]{1,0:T(4,128)S(1)}, s32[4,197]{1,0:T(4,128)}, u32[]{:S(2)}) copy-start(s32[4,197]{1,0:T(4,128)} %copy-done.40) | copy-start | bytes 9460
  290.9 38.5 %all-to-all-start.1 = ((bf16[16,4,32,384]{3,2,1,0:T(8,128)(2,1)}), bf16[16,4,32,384]{3,2,1,0:T(8,128)(2,1)}, u32[]{:S(2)}, u32[]{:S(2)}) async-start(bf16[16,4,32,384]{3,2,1,0:T(8,128)(2,1)} %bitcast.25), calls=%async_computation.1 | async-start | bytes 3145728 | tf_op jit(solution)/shard_map/all_to_all | solution.py:89
  297.4 4.0 copy-start.12
  297.4 4.0 copy-start.21
  301.2 3.9 copy-start.25
  302.0 15.9 %copy-start.2 = (f32[4,197,384]{2,1,0:T(8,128)}, f32[4,197,384]{2,1,0:T(8,128)S(1)}, u32[]{:S(2)}) copy-start(f32[4,197,384]{2,1,0:T(8,128)S(1)} %multiply_add_fusion) | copy-start | bytes 3631108
  302.0 7.1 %slice-start = ((s8[4915200]{0:T(1024)(128)(4,1)}), s8[720896]{0:T(1024)(128)(4,1)S(1)}, s32[]{:S(2)}) async-start(s8[4915200]{0:T(1024)(128)(4,1)} %bitcast.217), calls=%async_computation.7 | async-start | bytes 1441792
  305.0 4.1 %slice-start.1 = ((s8[4915200]{0:T(1024)(128)(4,1)}), s8[4194304]{0:T(1024)(128)(4,1)S(1)}, s32[]{:S(2)}) async-start(s8[4915200]{0:T(1024)(128)(4,1)} %bitcast.217), calls=%async_computation.8 | async-start | bytes 8388608
  309.1 1.7 copy-start.4
  310.8 1.5 copy-start.20
  313.2 1.1 copy-start.9
  313.2 1.5 copy-start.23
  313.2 1.5 copy-start.29
  313.2 1.5 copy-start.33
  313.2 1.5 copy-start.35
  314.1 3.7 copy-start.19
  314.7 3.8 copy-start.43
  317.7 3.3 copy-start.22
  329.4 36.1 %all-to-all-start.4 = ((bf16[16,24,1664]{2,1,0:T(8,128)(2,1)}), bf16[16,24,1664]{2,1,0:T(8,128)(2,1)}, u32[]{:S(2)}, u32[]{:S(2)}) async-start(bf16[16,24,1664]{2,1,0:T(8,128)(2,1)} %bitcast.55), calls=%async_computation.4 | async-start | bytes 2555904 | tf_op jit(solution)/shard_map/all_to_all | solution.py:188
  338.6 53.3 %all-reduce.4.cloned.1.call-start = ((), (), s32[]{:S(2)}) async-start(), calls=%async_computation.6 | async-start | bytes 319488 | tf_op jit(solution)/shard_map/psum | solution.py:190
  338.6 14.1 %copy-start.13 = (f32[4,197,384]{2,1,0:T(8,128)S(1)}, f32[4,197,384]{2,1,0:T(8,128)}, u32[]{:S(2)}) copy-start(f32[4,197,384]{2,1,0:T(8,128)} %copy-done.10) | copy-start | bytes 3631108
  352.7 45.0 %copy-start.1 = (bf16[2,384,1536]{2,1,0:T(8,128)(2,1)S(1)}, bf16[2,384,1536]{2,1,0:T(8,128)(2,1)}, u32[]{:S(2)}) copy-start(bf16[2,384,1536]{2,1,0:T(8,128)(2,1)} %param.25) | copy-start | bytes 7077892
Sparse Core Ops, SparseCore 0:
  12.1 56.3 all-gather.1
  367.8 24.0 all-reduce.3
